TPU v7x, 256 devices: a whole 4x4x8 slice. The times are simulated.
256 devices in a mesh: ctx: 32 (over y, x, core), head: 8 (over z).
Axes of the slice: x: 4, y: 4, z: 8, core: 2. Of those that a mesh axis runs over, the one named last changes fastest.
Arguments:
- q_latent: bfloat16 [4096, 128, 512], P('ctx', 'head'), may hold values from -80 to 80
- q_rope: bfloat16 [4096, 8192], P('ctx', 'head'), may hold values from -80 to 80
- kv_latent: bfloat16 [4096, 16, 512], P('ctx', None, 'head'), may hold values from -6.5 to 6.5
- kv_rope: bfloat16 [4096, 1024], P('ctx'), may hold values from -6.5 to 6.5
- grad_out: bfloat16 [4096, 128, 512], P('ctx', 'head'), may hold values from -6 to 6
- block_slot: int32 [4096], replicated, may hold values from 0 to 4095, as said below
- pool: int32 [32, 32, 2], P('ctx'), may hold values from -1 to 4095, as said below
- selected: int32 [4096, 32], P('ctx'), may hold values from 0 to 63, as said below
Outputs:
- d_q_latent: bfloat16 [4096, 128, 512], P('ctx', 'head')
- d_q_rope: bfloat16 [4096, 8192], P('ctx', 'head')
- d_kv_latent: bfloat16 [4096, 16, 512], P('ctx', None, 'head')
- d_kv_rope: bfloat16 [4096, 1024], P('ctx', 'head')
Inputs may be any that keep to these rules, and one draw needn't show every extreme that they name: `block_slot`: a permutation of the context blocks; storage rows r * 128 to (r + 1) * 128 - 1 belong to ctx index r. pool[s, o] lists distinct blocks owned by ctx index o (block_slot // 128 == o) that queries of shard s select, filled slots first, then -1; no block appears twice in pool[s]; each pool[s, o] has 1 or 2 filled slots, and some owner o has all 2 slots filled in pool[s, o] for every s. selected[t] holds 32 distinct positions of filled slots in pool[t // 128] read as 64 slots in a row.
All inputs are finite; a program needn't handle non-finite values.
Results may differ from a plain program's by a relative error of at most 0.0051.
Values may be sent and summed in bfloat16 or wider, within the bound.
A program may use at most 128 MiB of HBM per device.

v0:
```python
import jax
import jax.numpy as jnp
from jax import lax
from jax.sharding import PartitionSpec as P

SCALE = 192.0 ** (-0.5)


def local(q_latent, q_rope, kv_latent, kv_rope, grad_out, block_slot, pool, selected):
    shards = lax.axis_size("ctx")
    owned = kv_latent.shape[0]
    block_len = kv_latent.shape[1]
    cap = pool.shape[2]
    slots = shards * cap
    queries, heads_here, latent = q_latent.shape
    rope = q_rope.shape[1] // heads_here
    wanted = pool[0]
    filled = wanted >= 0
    table = jnp.arange(block_slot.shape[0], dtype=jnp.int32)
    stored = jnp.sum(
        jnp.where(wanted[:, :, None] == table[None, None, :], block_slot[None, None, :], 0), axis=2
    )
    offset = jnp.arange(shards, dtype=jnp.int32)[:, None] * owned
    local_rows = jnp.where(filled, stored - offset, 0)
    requests = lax.all_to_all(local_rows, "ctx", split_axis=0, concat_axis=0, tiled=True)
    full_latent = lax.all_gather(kv_latent, "head", axis=2, tiled=True)
    pool_latent, pool_rope = (
        lax.all_to_all(full_latent[requests], "ctx", split_axis=0, concat_axis=0, tiled=True),
        lax.all_to_all(kv_rope[requests], "ctx", split_axis=0, concat_axis=0, tiled=True),
    )
    width_keys = slots * block_len
    keys_latent = pool_latent.reshape(width_keys, latent)
    keys_rope = pool_rope.reshape(width_keys, rope)
    q_rot = q_rope.reshape(queries, heads_here, rope)
    chosen = jnp.any(
        selected[:, :, None] == jnp.arange(slots, dtype=jnp.int32)[None, None, :], axis=1
    )
    visible = jnp.repeat(chosen, block_len, axis=1)
    step_rows = 64
    count = queries // step_rows

    def one_block(carry, item):
        acc_latent, acc_rope = carry
        q_lat, q_rt, cotan, seen = item
        scores = jnp.einsum("qhl,kl->qhk", q_lat, keys_latent, preferred_element_type=jnp.float32)
        scores = (
            scores + jnp.einsum("qhr,kr->qhk", q_rt, keys_rope, preferred_element_type=jnp.float32)
        ) * SCALE
        scores = jnp.where(seen[:, None, :], scores, -jnp.inf)
        peak = jnp.max(scores, axis=2, keepdims=True)
        weights = jnp.exp(scores - peak)
        probs = weights / jnp.sum(weights, axis=2, keepdims=True)
        dprobs = jnp.einsum("qhl,kl->qhk", cotan, keys_latent, preferred_element_type=jnp.float32)
        delta = jnp.sum(probs * dprobs, axis=2, keepdims=True)
        dscores = (probs * (dprobs - delta) * SCALE).astype(jnp.bfloat16)
        probs_low = probs.astype(jnp.bfloat16)
        grad_qlat = jnp.einsum(
            "qhk,kl->qhl", dscores, keys_latent, preferred_element_type=jnp.float32
        ).astype(jnp.bfloat16)
        grad_qrot = jnp.einsum(
            "qhk,kr->qhr", dscores, keys_rope, preferred_element_type=jnp.float32
        ).astype(jnp.bfloat16)
        acc_latent = acc_latent + jnp.einsum(
            "qhk,qhl->kl", dscores, q_lat, preferred_element_type=jnp.float32
        )
        acc_latent = acc_latent + jnp.einsum(
            "qhk,qhl->kl", probs_low, cotan, preferred_element_type=jnp.float32
        )
        acc_rope = acc_rope + jnp.einsum(
            "qhk,qhr->kr", dscores, q_rt, preferred_element_type=jnp.float32
        )
        return ((acc_latent, acc_rope), (grad_qlat, grad_qrot))

    start = (
        jnp.zeros((width_keys, latent), jnp.float32),
        jnp.zeros((width_keys, rope), jnp.float32),
    )
    items = (
        q_latent.reshape(count, step_rows, heads_here, latent),
        q_rot.reshape(count, step_rows, heads_here, rope),
        grad_out.reshape(count, step_rows, heads_here, latent),
        visible.reshape(count, step_rows, width_keys),
    )
    (grad_latent, grad_rope), (part_qlat, part_qrot) = lax.scan(one_block, start, items)
    d_q_latent = part_qlat.reshape(queries, heads_here, latent)
    d_q_rope = part_qrot.reshape(queries, heads_here * rope)
    grad_latent = grad_latent.reshape(shards, cap, block_len, latent)
    grad_rope = grad_rope.reshape(shards, cap, block_len * rope)
    flat_requests = requests.reshape(slots)
    got_latent, got_rope = (
        lax.all_to_all(grad_latent, "ctx", split_axis=0, concat_axis=0, tiled=True),
        lax.all_to_all(grad_rope, "ctx", split_axis=0, concat_axis=0, tiled=True),
    )
    width = got_latent.shape[3]
    summed_latent = (
        jnp.zeros((owned, block_len, width), jnp.float32)
        .at[flat_requests]
        .add(got_latent.reshape(slots, block_len, width))
    )
    summed_rope = (
        jnp.zeros((owned, got_rope.shape[2]), jnp.float32)
        .at[flat_requests]
        .add(got_rope.reshape(slots, got_rope.shape[2]))
    )
    out_latent, out_rope = (
        lax.psum_scatter(summed_latent, "head", scatter_dimension=2, tiled=True),
        lax.psum_scatter(summed_rope, "head", scatter_dimension=1, tiled=True),
    )
    return (d_q_latent, d_q_rope, out_latent.astype(jnp.bfloat16), out_rope.astype(jnp.bfloat16))


def solution(mesh):
    return jax.shard_map(
        local,
        mesh=mesh,
        in_specs=(
            P("ctx", "head", None),
            P("ctx", "head"),
            P("ctx", None, "head"),
            P("ctx", None),
            P("ctx", "head", None),
            P(),
            P("ctx", None, None),
            P("ctx", None),
        ),
        out_specs=(
            P("ctx", "head", None),
            P("ctx", "head"),
            P("ctx", None, "head"),
            P("ctx", "head"),
        ),
        check_vma=False,
    )
```

profile of v0, /device:TPU:1, one launch (start us, length us, event | category | flops | bytes accessed | tf_op | source)
XLA Modules:
  0.0 346.8 jit_solution(17000684935951401226)
XLA Ops:
  10.9 15.3 %all_to_all.29 = s32[32,1,2]{2,1,0:T(1,128)S(1)} all-to-all(s32[32,1,2]{2,1,0:T(1,128)S(1)} %copy.52), channel_id=1, replica_groups=mesh['ctx'=32,'head'=8] {'ctx'}, dimensions={0} | all-to-all | bytes 512 | tf_op jit(solution)/shard_map/all_to_all | solution.py:25
  28.3 4.2 %all-to-all-start.2 = ((bf16[32,2,1024]{2,1,0:T(2,128)(2,1)}), bf16[32,2,1024]{2,1,0:T(2,128)(2,1)S(1)}, u32[]{:S(2)}, u32[]{:S(2)}) async-start(bf16[32,2,1024]{2,1,0:T(2,128)(2,1)} %reshape.173), calls=%async_computation.2 | async-start | bytes 262144 | tf_op jit(solution)/shard_map/all_to_all | solution.py:29
  32.5 19.2 %all-gather.2.cloned.1.call-done = bf16[128,16,512]{0,1,2:T(8,128)(2,1)} async-done(((bf16[128,16,64]{0,1,2:T(8,128)(2,1)}), bf16[128,16,512]{0,1,2:T(8,128)(2,1)}) %all-gather.2.cloned.1.call-update) | async-done | bytes 2097168 | tf_op jit(solution)/shard_map/all_gather | solution.py:26
  51.6 4.8 %copy.55 = bf16[128,16,512]{2,1,0:T(8,128)(2,1)} copy(bf16[128,16,512]{0,1,2:T(8,128)(2,1)} %all-gather.2.cloned.1.call-done) | data formatting | bytes 4194304 | tf_op jit(solution)/shard_map/all_gather | solution.py:26
  56.4 3.3 gather_fusion
  59.8 11.2 %all-to-all-start.1 = ((bf16[32,2,16,512]{3,2,1,0:T(8,128)(2,1)}), bf16[32,2,16,512]{3,2,1,0:T(8,128)(2,1)S(1)}, u32[]{:S(2)}, u32[]{:S(2)}) async-start(bf16[32,2,16,512]{3,2,1,0:T(8,128)(2,1)} %bitcast.115), calls=%async_computation.1 | async-start | bytes 2097152 | tf_op jit(solution)/shard_map/all_to_all | solution.py:28
  71.9 2.7 reshape_reshape.6
  74.6 2.0 copy.56
  76.6 2.2 reshape_reshape.7
  80.7 7.5 %all-to-all-done.1 = bf16[32,2,16,512]{3,2,1,0:T(8,128)(2,1)S(1)} async-done(((bf16[32,2,16,512]{3,2,1,0:T(8,128)(2,1)}), bf16[32,2,16,512]{3,2,1,0:T(8,128)(2,1)S(1)}, u32[]{:S(2)}, u32[]{:S(2)}) %all-to-all-start.1) | async-done | bytes 1048608 | tf_op jit(solution)/shard_map/all_to_all | solution.py:28
  88.2 135.3 %while.17 = (s32[]{:T(128)}, f32[1024,512]{1,0:T(8,128)}, f32[1024,64]{0,1:T(8,128)}, bf16[2,64,16,512]{3,2,1,0:T(8,128)(2,1)}, bf16[2,64,16,64]{3,2,1,0:T(8,128...) while((s32[]{:T(128)}, f32[1024,512]{1,0:T(8,128)}, ...), condition=%wide.region_6.7_spmd.clone, body=%wide.region_2.6_spmd.clone.sunk | while | flops 5811416064 | bytes 145199344 | solution.py:84
  91.5 3.8 %fusion.104 = (f32[64,16]{1,0:T(8,128)}, f32[64,16,1024]{2,1,0:T(8,128)}) fusion(f32[64,16,1024]{2,1,0:T(8,128)S(1)} %multiply_select_fusion.2), kind=kOutput, calls=%fused_computation.71.clone.1 | output fusion | flops 2098175 | bytes 8392704 | tf_op jit(solution)/shard_map/while/body/eval_jaxpr/sub | solution.py:51
  95.3 7.3 %fusion.105 = f32[1024,512,1]{1,0,2:T(8,128)} fusion(bf16[2,64,16,512]{3,2,1,0:T(8,128)(2,1)S(1)} %get-tuple-element.280, s32[]{:T(128)S(6)} %copy.68, f32[64,16]{1,0:T(8,128)} %get-tuple-element.242, f32[64,16,1024]{2,1,0:T(8,128)} %copy-done.1), kind=kOutput, calls=%fused_computation.13.clone.1 | convolution fusion | flops 1076889600 | bytes 11567108 | tf_op jit(solution)/shard_map/while/body/eval_jaxpr/qhk,qhl->kl/dot_general | solution.py:66
  102.6 3.3 fusion.106
  105.8 14.2 %bitcast_add_fusion.3 = f32[1024,512]{1,0:T(8,128)} fusion(f32[1024,512,1]{1,0,2:T(8,128)} %fusion.105, f32[1024,512]{1,0:T(8,128)} %get-tuple-element.258, pred[]{:T(512)S(6)} %compare.3, bf16[2,64,16,512]{3,2,1,0:T(8,128)(2,1)} %get-tuple-element.276, s32[]{:T(128)S(6)} %copy.68, f32[64,16,1024]{2,1,0:T(8,128)} %fusion.106, ...), kind=kOutput, calls=%fused_computation.11.clone.1 | convolution fusion | flops 1082656768 | bytes 24182788 | tf_op jit(solution)/shard_map/while/body/eval_jaxpr/qhk,qhl->kl/dot_general | solution.py:63
  120.0 12.3 %fusion.107 = f32[1024,64]{0,1:T(8,128)} fusion(f32[64,16,1024]{2,1,0:T(8,128)} %fusion.106, f32[1024,64]{0,1:T(8,128)} %get-tuple-element.259, bf16[2,64,16,64]{3,2,1,0:T(8,128)(2,1)} %get-tuple-element.278, s32[]{:T(128)S(6)} %copy.68, pred[]{:T(512)S(6)} %compare.3, f32[64,16,1024]{2,1,0:T(8,128)} %get-tuple-element.243, ...), kind=kOutput, calls=%fused_computation.21.clone.1 | convolution fusion | flops 141690880 | bytes 17629188 | tf_op jit(solution)/shard_map/while/body/eval_jaxpr/qhk,qhr->kr/dot_general | solution.py:69
  132.3 11.3 %fusion.108 = bf16[2,64,16,512]{3,2,1,0:T(8,128)(2,1)} fusion(bf16[2,64,16,512]{3,2,1,0:T(8,128)(2,1)} %get-tuple-element.260, s32[]{:T(128)S(6)} %copy.68, bf16[1024,512]{1,0:T(8,128)(2,1)S(1)} %get-tuple-element.277, f32[64,16,1024]{2,1,0:T(8,128)} %fusion.106, f32[64,16,1024]{2,1,0:T(8,128)} %get-tuple-element.243, f32[64,16]{1,0:T(8,128)} %get-tuple-element.242), kind=kOutput, calls=%fused_computation.18.clone.1 | convolution fusion | flops 1081608192 | bytes 18939908 | tf_op jit(solution)/shard_map/while/body/eval_jaxpr/qhk,kl->qhl/dot_general | solution.py:57
  143.7 11.9 %fusion.109 = bf16[2,64,16,64]{3,2,1,0:T(8,128)(2,1)} fusion(bf16[2,64,16,64]{3,2,1,0:T(8,128)(2,1)} %get-tuple-element.261, s32[]{:T(128)S(6)} %copy.68, f32[64,16,1024]{2,1,0:T(8,128)} %fusion.106, bf16[1024,64]{0,1:T(8,128)(2,1)S(1)} %get-tuple-element.279, f32[64,16,1024]{2,1,0:T(8,128)} %get-tuple-element.243, f32[64,16]{1,0:T(8,128)} %get-tuple-element.242), kind=kOutput, calls=%fused_computation.23.clone.1 | convolution fusion | flops 141625344 | bytes 17235972 | tf_op jit(solution)/shard_map/while/body/eval_jaxpr/qhk,kr->qhr/dot_general | solution.py:60
  158.8 3.8 %fusion.104 = (f32[64,16]{1,0:T(8,128)}, f32[64,16,1024]{2,1,0:T(8,128)}) fusion(f32[64,16,1024]{2,1,0:T(8,128)S(1)} %multiply_select_fusion.2), kind=kOutput, calls=%fused_computation.71.clone.1 | output fusion | flops 2098175 | bytes 8392704 | tf_op jit(solution)/shard_map/while/body/eval_jaxpr/sub | solution.py:51
  162.6 7.3 %fusion.105 = f32[1024,512,1]{1,0,2:T(8,128)} fusion(bf16[2,64,16,512]{3,2,1,0:T(8,128)(2,1)S(1)} %get-tuple-element.280, s32[]{:T(128)S(6)} %copy.68, f32[64,16]{1,0:T(8,128)} %get-tuple-element.242, f32[64,16,1024]{2,1,0:T(8,128)} %copy-done.1), kind=kOutput, calls=%fused_computation.13.clone.1 | convolution fusion | flops 1076889600 | bytes 11567108 | tf_op jit(solution)/shard_map/while/body/eval_jaxpr/qhk,qhl->kl/dot_general | solution.py:66
  169.9 3.3 fusion.106
  173.2 14.8 %bitcast_add_fusion.3 = f32[1024,512]{1,0:T(8,128)} fusion(f32[1024,512,1]{1,0,2:T(8,128)} %fusion.105, f32[1024,512]{1,0:T(8,128)} %get-tuple-element.258, pred[]{:T(512)S(6)} %compare.3, bf16[2,64,16,512]{3,2,1,0:T(8,128)(2,1)} %get-tuple-element.276, s32[]{:T(128)S(6)} %copy.68, f32[64,16,1024]{2,1,0:T(8,128)} %fusion.106, ...), kind=kOutput, calls=%fused_computation.11.clone.1 | convolution fusion | flops 1082656768 | bytes 24182788 | tf_op jit(solution)/shard_map/while/body/eval_jaxpr/qhk,qhl->kl/dot_general | solution.py:63
  187.9 12.3 %fusion.107 = f32[1024,64]{0,1:T(8,128)} fusion(f32[64,16,1024]{2,1,0:T(8,128)} %fusion.106, f32[1024,64]{0,1:T(8,128)} %get-tuple-element.259, bf16[2,64,16,64]{3,2,1,0:T(8,128)(2,1)} %get-tuple-element.278, s32[]{:T(128)S(6)} %copy.68, pred[]{:T(512)S(6)} %compare.3, f32[64,16,1024]{2,1,0:T(8,128)} %get-tuple-element.243, ...), kind=kOutput, calls=%fused_computation.21.clone.1 | convolution fusion | flops 141690880 | bytes 17629188 | tf_op jit(solution)/shard_map/while/body/eval_jaxpr/qhk,qhr->kr/dot_general | solution.py:69
  200.3 11.3 %fusion.108 = bf16[2,64,16,512]{3,2,1,0:T(8,128)(2,1)} fusion(bf16[2,64,16,512]{3,2,1,0:T(8,128)(2,1)} %get-tuple-element.260, s32[]{:T(128)S(6)} %copy.68, bf16[1024,512]{1,0:T(8,128)(2,1)S(1)} %get-tuple-element.277, f32[64,16,1024]{2,1,0:T(8,128)} %fusion.106, f32[64,16,1024]{2,1,0:T(8,128)} %get-tuple-element.243, f32[64,16]{1,0:T(8,128)} %get-tuple-element.242), kind=kOutput, calls=%fused_computation.18.clone.1 | convolution fusion | flops 1081608192 | bytes 18939908 | tf_op jit(solution)/shard_map/while/body/eval_jaxpr/qhk,kl->qhl/dot_general | solution.py:57
  211.6 11.9 %fusion.109 = bf16[2,64,16,64]{3,2,1,0:T(8,128)(2,1)} fusion(bf16[2,64,16,64]{3,2,1,0:T(8,128)(2,1)} %get-tuple-element.261, s32[]{:T(128)S(6)} %copy.68, f32[64,16,1024]{2,1,0:T(8,128)} %fusion.106, bf16[1024,64]{0,1:T(8,128)(2,1)S(1)} %get-tuple-element.279, f32[64,16,1024]{2,1,0:T(8,128)} %get-tuple-element.243, f32[64,16]{1,0:T(8,128)} %get-tuple-element.242), kind=kOutput, calls=%fused_computation.23.clone.1 | convolution fusion | flops 141625344 | bytes 17235972 | tf_op jit(solution)/shard_map/while/body/eval_jaxpr/qhk,kr->qhr/dot_general | solution.py:60
  224.9 12.4 %all_to_all.30 = f32[32,2,1024]{2,1,0:T(2,128)S(1)} all-to-all(f32[32,2,1024]{2,1,0:T(2,128)S(1)} %reshape.162), channel_id=1, replica_groups=mesh['ctx'=32,'head'=8] {'ctx'}, dimensions={0} | all-to-all | bytes 524288 | tf_op jit(solution)/shard_map/all_to_all | solution.py:92
  237.3 3.9 %all-to-all-start.3 = ((f32[32,2,16,512]{3,2,1,0:T(8,128)}), f32[32,2,16,512]{3,2,1,0:T(8,128)S(1)}, u32[]{:S(2)}, u32[]{:S(2)}) async-start(f32[32,2,16,512]{3,2,1,0:T(8,128)} %bitcast.116), calls=%async_computation.3 | async-start | bytes 4194304 | tf_op jit(solution)/shard_map/all_to_all | solution.py:91
  244.8 24.4 %all-to-all-done.3 = f32[32,2,16,512]{3,2,1,0:T(8,128)S(1)} async-done(((f32[32,2,16,512]{3,2,1,0:T(8,128)}), f32[32,2,16,512]{3,2,1,0:T(8,128)S(1)}, u32[]{:S(2)}, u32[]{:S(2)}) %all-to-all-start.3) | async-done | bytes 2097184 | tf_op jit(solution)/shard_map/all_to_all | solution.py:91
  269.2 2.5 broadcast_in_dim.77
  271.7 9.0 %scatter_fusion = f32[128,16,512]{2,1,0:T(8,128)} fusion(f32[128,16,512]{2,1,0:T(8,128)} %broadcast_in_dim.77, s32[64]{0:T(128)S(1)} %fusion.56, f32[64,16,512]{2,1,0:T(8,128)S(1)} %bitcast.114), kind=kCustom, calls=%fused_computation.2 | custom fusion | flops 524288 | bytes 6291712 | tf_op jit(solution)/shard_map/scatter-add | solution.py:98
  280.7 5.8 %copy.58 = f32[128,16,512]{0,1,2:T(8,128)} copy(f32[128,16,512]{2,1,0:T(8,128)} %scatter_fusion) | data formatting | bytes 8388608 | tf_op jit(solution)/shard_map/scatter-add | solution.py:98
  290.1 48.3 %reduce-scatter.3.cloned.1.call-done = f32[128,16,64]{0,1,2:T(8,128)} async-done(((f32[128,16,512]{0,1,2:T(8,128)}), f32[128,16,64]{0,1,2:T(8,128)}) %reduce-scatter.3.cloned.1.call-update) | async-done | bytes 524304 | tf_op jit(solution)/shard_map/reduce_scatter | solution.py:106
  (70 shorter events, 25.4 us)
Async XLA Ops:
  7.2 19.7 %copy-start = (bf16[128,1024]{1,0:T(8,128)(2,1)S(1)}, bf16[128,1024]{1,0:T(8,128)(2,1)}, u32[]{:S(2)}) copy-start(bf16[128,1024]{1,0:T(8,128)(2,1)} %param.13) | copy-start | bytes 786436
  7.2 44.4 %all-gather.2.cloned.1.call-start = ((), (), s32[]{:S(2)}) async-start(), calls=%async_computation.7 | async-start | bytes 2359296 | tf_op jit(solution)/shard_map/all_gather | solution.py:26
  26.2 0.6 copy-start.6
  28.3 31.5 %all-to-all-start.2 = ((bf16[32,2,1024]{2,1,0:T(2,128)(2,1)}), bf16[32,2,1024]{2,1,0:T(2,128)(2,1)S(1)}, u32[]{:S(2)}, u32[]{:S(2)}) async-start(bf16[32,2,1024]{2,1,0:T(2,128)(2,1)} %reshape.173), calls=%async_computation.2 | async-start | bytes 262144 | tf_op jit(solution)/shard_map/all_to_all | solution.py:29
  32.4 38.6 %copy-start.8 = (s32[128,32]{0,1:T(8,128)S(1)}, s32[128,32]{0,1:T(8,128)}, u32[]{:S(2)}) copy-start(s32[128,32]{0,1:T(8,128)} %param.17) | copy-start | bytes 49156
  56.4 31.8 %copy-start.2 = (bf16[128,16,512]{2,1,0:T(8,128)(2,1)S(1)}, bf16[128,16,512]{2,1,0:T(8,128)(2,1)}, u32[]{:S(2)}) copy-start(bf16[128,16,512]{2,1,0:T(8,128)(2,1)} %param.14) | copy-start | bytes 6291460
  59.8 28.4 %all-to-all-start.1 = ((bf16[32,2,16,512]{3,2,1,0:T(8,128)(2,1)}), bf16[32,2,16,512]{3,2,1,0:T(8,128)(2,1)S(1)}, u32[]{:S(2)}, u32[]{:S(2)}) async-start(bf16[32,2,16,512]{3,2,1,0:T(8,128)(2,1)} %bitcast.115), calls=%async_computation.1 | async-start | bytes 2097152 | tf_op jit(solution)/shard_map/all_to_all | solution.py:28
  88.2 1.8 copy-start.4
  88.2 1.8 copy-start.3
  91.5 3.8 %copy-start.1 = (f32[64,16,1024]{2,1,0:T(8,128)}, f32[64,16,1024]{2,1,0:T(8,128)S(1)}, u32[]{:S(2)}) copy-start(f32[64,16,1024]{2,1,0:T(8,128)S(1)} %multiply_select_fusion.2) | copy-start | bytes 12582916 | tf_op jit(solution)/shard_map/while
  155.5 1.8 copy-start.4
  155.6 1.8 copy-start.3
  158.8 3.8 %copy-start.1 = (f32[64,16,1024]{2,1,0:T(8,128)}, f32[64,16,1024]{2,1,0:T(8,128)S(1)}, u32[]{:S(2)}) copy-start(f32[64,16,1024]{2,1,0:T(8,128)S(1)} %multiply_select_fusion.2) | copy-start | bytes 12582916 | tf_op jit(solution)/shard_map/while
  223.5 18.3 %copy-start.7 = (s32[32,1,2]{2,1,0:T(1,128)S(1)}, s32[32,1,2]{2,1,0:T(1,128)}, u32[]{:S(2)}) copy-start(s32[32,1,2]{2,1,0:T(1,128)} %copy-done.6) | copy-start | bytes 772
  237.3 31.9 %all-to-all-start.3 = ((f32[32,2,16,512]{3,2,1,0:T(8,128)}), f32[32,2,16,512]{3,2,1,0:T(8,128)S(1)}, u32[]{:S(2)}, u32[]{:S(2)}) async-start(f32[32,2,16,512]{3,2,1,0:T(8,128)} %bitcast.116), calls=%async_computation.3 | async-start | bytes 4194304 | tf_op jit(solution)/shard_map/all_to_all | solution.py:91
  241.2 47.4 %reduce-scatter.5.cloned.1.call-start = ((), (), s32[]{:S(2)}) async-start(), calls=%async_computation.9 | async-start | bytes 589824 | tf_op jit(solution)/shard_map/reduce_scatter | solution.py:107
  244.7 93.6 %reduce-scatter.3.cloned.1.call-start = ((), (), s32[]{:S(2)}) async-start(), calls=%async_computation.8 | async-start | bytes 4718592 | tf_op jit(solution)/shard_map/reduce_scatter | solution.py:106
  286.6 1.0 copy-start.5
Sparse Core Ops, SparseCore 0:
  10.4 41.1 all-gather.1
  244.9 31.8 reduce-scatter.4
  286.7 51.6 reduce-scatter.2
where the time goes:
time: 348 us; the launch traced here: 347 us
  matrix products  128 us (37%)
  waiting for transfers between devices  99.3 us (29%)
  local copies, waits for them, and re-layouts  35.1 us (10%)
  blocking collectives  27.7 us (8%)
  other arithmetic  23.6 us (7%)
  starting transfers between devices  19.4 us (6%)
  between operations  13.9 us (4%)
    reduce_scatter x1, waiting for transfers between devices, local(): lax.psum_scatter(summed_latent, 'head', scatter_dimension=2, tiled=True)  48.3 us
    dot_general x2, matrix products, one_block(): jnp.einsum('qhk,qhl->kl', dscores, q_lat, preferred_element_type=jnp.floa...  28.9 us
    dot_general x2, matrix products, one_block(): jnp.einsum('qhk,qhr->kr', dscores, q_rt, preferred_element_type=jnp.float32)  24.7 us
    all_to_all x1, waiting for transfers between devices, local(): lax.all_to_all(grad_latent, 'ctx', split_axis=0, concat_axis=0, tiled=True)  24.4 us
    dot_general x2, matrix products, one_block(): jnp.einsum('qhk,kr->qhr', dscores, keys_rope, preferred_element_type=jnp....  23.7 us
    dot_general x2, matrix products, one_block(): jnp.einsum('qhk,kl->qhl', dscores, keys_latent, preferred_element_type=jn...  22.7 us
    all_gather x1, waiting for transfers between devices, local(): full_latent = lax.all_gather(kv_latent, 'head', axis=2, tiled=True)  19.2 us
    all_to_all x1, blocking collectives, local(): lax.all_to_all(local_rows, 'ctx', split_axis=0, concat_axis=0, tiled=True)  15.3 us
  transfers between devices with their start and end apart: 6, of which 4 were waited for; matrix products, arithmetic and copies ran while one was open for 13% of the time, Pallas kernels for 0%

commit v1 on v0

--- a/solution.py
+++ b/solution.py
@@ -23,7 +23,9 @@
     offset = jnp.arange(shards, dtype=jnp.int32)[:, None] * owned
     local_rows = jnp.where(filled, stored - offset, 0)
     requests = lax.all_to_all(local_rows, "ctx", split_axis=0, concat_axis=0, tiled=True)
-    full_latent = lax.all_gather(kv_latent, "head", axis=2, tiled=True)
+    full_latent = jnp.concatenate(
+        lax.all_to_all(jnp.stack([kv_latent] * lax.axis_size("head")), "head", 0, 0), axis=2
+    )
     pool_latent, pool_rope = (
         lax.all_to_all(full_latent[requests], "ctx", split_axis=0, concat_axis=0, tiled=True),
         lax.all_to_all(kv_rope[requests], "ctx", split_axis=0, concat_axis=0, tiled=True),

time: 348 us -> 383 us (1.10)
  waiting for transfers between devices: 99.3 us -> 124 us
  starting transfers between devices: 19.4 us -> 26.9 us
    all_to_all x0 -> x1, waiting for transfers between devices: none -> 46.7 us  [local(): lax.all_to_all(jnp.stack([kv_latent] * lax.axis_size('head')), 'head', 0, 0)]
    all_gather x1 -> x0, waiting for transfers between devices: 19.2 us -> none  [local(): full_latent = lax.all_gather(kv_latent, 'head', axis=2, tiled=True)]
    all_to_all x0 -> x1, starting transfers between devices: none -> 8.19 us  [local(): lax.all_to_all(jnp.stack([kv_latent] * lax.axis_size('head')), 'head', 0, 0)]
    all_gather x1 -> x0, local copies, waits for them, and re-layouts: 4.82 us -> none  [local(): full_latent = lax.all_gather(kv_latent, 'head', axis=2, tiled=True)]
    reshape x0 -> x1, local copies, waits for them, and re-layouts: none -> 4.63 us  [local(): jnp.concatenate(lax.all_to_all(jnp.stack([kv_latent] * lax.axis_size('hea...]
  transfers between devices with their start and end apart: 6 -> 6, of which waited for: 4 -> 4; matrix products, arithmetic and copies ran while one was open for 13% -> 12% of each run, Pallas kernels for 0% -> 0%
where the time goes in v1:
time: 383 us; the launch traced here: 382 us
  matrix products  128 us (33%)
  waiting for transfers between devices  124 us (32%)
  local copies, waits for them, and re-layouts  37.1 us (10%)
  blocking collectives  27.7 us (7%)
  starting transfers between devices  26.9 us (7%)
  other arithmetic  24.3 us (6%)
  between operations  14.2 us (4%)
    all_to_all x1, waiting for transfers between devices, local(): lax.all_to_all(jnp.stack([kv_latent] * lax.axis_size('head')), 'head', 0, 0)  46.7 us
    reduce_scatter x1, waiting for transfers between devices, local(): lax.psum_scatter(summed_latent, 'head', scatter_dimension=2, tiled=True)  45.7 us
    dot_general x2, matrix products, one_block(): jnp.einsum('qhk,qhl->kl', dscores, q_lat, preferred_element_type=jnp.floa...  28.9 us
    dot_general x2, matrix products, one_block(): jnp.einsum('qhk,qhr->kr', dscores, q_rt, preferred_element_type=jnp.float32)  24.7 us
    all_to_all x1, waiting for transfers between devices, local(): lax.all_to_all(grad_latent, 'ctx', split_axis=0, concat_axis=0, tiled=True)  24.4 us
    dot_general x2, matrix products, one_block(): jnp.einsum('qhk,kr->qhr', dscores, keys_rope, preferred_element_type=jnp....  23.7 us
    dot_general x2, matrix products, one_block(): jnp.einsum('qhk,kl->qhl', dscores, keys_latent, preferred_element_type=jn...  22.7 us
    all_to_all x1, blocking collectives, local(): lax.all_to_all(local_rows, 'ctx', split_axis=0, concat_axis=0, tiled=True)  15.3 us
  transfers between devices with their start and end apart: 6, of which 4 were waited for; matrix products, arithmetic and copies ran while one was open for 12% of the time, Pallas kernels for 0%

profile of v1, /device:TPU:1, one launch (start us, length us, event | category | flops | bytes accessed | tf_op | source)
XLA Modules:
  0.0 381.5 jit_solution(14899378028248105288)
XLA Ops:
  9.0 15.3 %all_to_all.34 = s32[32,1,2]{2,1,0:T(1,128)S(1)} all-to-all(s32[32,1,2]{2,1,0:T(1,128)S(1)} %copy.61), channel_id=1, replica_groups=mesh['ctx'=32,'head'=8] {'ctx'}, dimensions={0} | all-to-all | bytes 512 | tf_op jit(solution)/shard_map/all_to_all | solution.py:25
  24.4 2.8 stack.2
  27.2 8.2 %all-to-all-start = ((bf16[8,128,16,64]{1,3,2,0:T(8,128)(2,1)}), bf16[8,128,16,64]{1,3,2,0:T(8,128)(2,1)S(1)}, u32[]{:S(2)}, u32[]{:S(2)}) async-start(bf16[8,128,16,64]{1,3,2,0:T(8,128)(2,1)} %stack.2), calls=%async_computation | async-start | bytes 4194304 | tf_op jit(solution)/shard_map/all_to_all | solution.py:27
  37.1 46.7 %all-to-all-done = bf16[8,128,16,64]{1,3,2,0:T(8,128)(2,1)S(1)} async-done(((bf16[8,128,16,64]{1,3,2,0:T(8,128)(2,1)}), bf16[8,128,16,64]{1,3,2,0:T(8,128)(2,1)S(1)}, u32[]{:S(2)}, u32[]{:S(2)}) %all-to-all-start) | async-done | bytes 2097184 | tf_op jit(solution)/shard_map/all_to_all | solution.py:27
  83.8 7.2 %all-to-all-start.3 = ((bf16[32,2,1024]{2,1,0:T(2,128)(2,1)}), bf16[32,2,1024]{2,1,0:T(2,128)(2,1)S(1)}, u32[]{:S(2)}, u32[]{:S(2)}) async-start(bf16[32,2,1024]{2,1,0:T(2,128)(2,1)} %reshape.183), calls=%async_computation.3 | async-start | bytes 262144 | tf_op jit(solution)/shard_map/all_to_all | solution.py:31
  92.6 4.6 %copy.64 = bf16[128,16,512]{2,1,0:T(8,128)(2,1)} copy(bf16[128,16,512]{0,2,1:T(8,128)(2,1)} %bitcast.118) | data formatting | bytes 4194304 | tf_op jit(solution)/shard_map/reshape | solution.py:26
  97.2 3.3 gather_fusion
  100.6 7.5 %all-to-all-start.2 = ((bf16[32,2,16,512]{3,2,1,0:T(8,128)(2,1)}), bf16[32,2,16,512]{3,2,1,0:T(8,128)(2,1)S(1)}, u32[]{:S(2)}, u32[]{:S(2)}) async-start(bf16[32,2,16,512]{3,2,1,0:T(8,128)(2,1)} %bitcast.119), calls=%async_computation.2 | async-start | bytes 2097152 | tf_op jit(solution)/shard_map/all_to_all | solution.py:30
  109.7 2.7 reshape_reshape.6
  118.5 6.7 %all-to-all-done.2 = bf16[32,2,16,512]{3,2,1,0:T(8,128)(2,1)S(1)} async-done(((bf16[32,2,16,512]{3,2,1,0:T(8,128)(2,1)}), bf16[32,2,16,512]{3,2,1,0:T(8,128)(2,1)S(1)}, u32[]{:S(2)}, u32[]{:S(2)}) %all-to-all-start.2) | async-done | bytes 1048608 | tf_op jit(solution)/shard_map/all_to_all | solution.py:30
  125.2 135.3 %while.17 = (s32[]{:T(128)}, f32[1024,512]{1,0:T(8,128)}, f32[1024,64]{0,1:T(8,128)}, bf16[2,64,16,512]{3,2,1,0:T(8,128)(2,1)}, bf16[2,64,16,64]{3,2,1,0:T(8,128...) while((s32[]{:T(128)}, f32[1024,512]{1,0:T(8,128)}, ...), condition=%wide.region_6.7_spmd.clone, body=%wide.region_2.6_spmd.clone.sunk | while | flops 5811416064 | bytes 145199344 | solution.py:86
  128.5 3.8 fusion.104
  132.3 7.3 %fusion.105 = f32[1024,512,1]{1,0,2:T(8,128)} fusion(bf16[2,64,16,512]{3,2,1,0:T(8,128)(2,1)S(1)} %get-tuple-element.295, s32[]{:T(128)S(6)} %copy.77, f32[64,16]{1,0:T(8,128)} %get-tuple-element.257, f32[64,16,1024]{2,1,0:T(8,128)} %copy-done.1), kind=kOutput, calls=%fused_computation.13.clone.1 | convolution fusion | flops 1076889600 | bytes 11567108 | tf_op jit(solution)/shard_map/while/body/eval_jaxpr/qhk,qhl->kl/dot_general | solution.py:68
  139.6 3.3 fusion.106
  142.9 14.2 %bitcast_add_fusion.3 = f32[1024,512]{1,0:T(8,128)} fusion(f32[1024,512,1]{1,0,2:T(8,128)} %fusion.105, f32[1024,512]{1,0:T(8,128)} %get-tuple-element.273, pred[]{:T(512)S(6)} %compare.3, bf16[2,64,16,512]{3,2,1,0:T(8,128)(2,1)} %get-tuple-element.291, s32[]{:T(128)S(6)} %copy.77, f32[64,16,1024]{2,1,0:T(8,128)} %fusion.106, ...), kind=kOutput, calls=%fused_computation.11.clone.1 | convolution fusion | flops 1082656768 | bytes 24182788 | tf_op jit(solution)/shard_map/while/body/eval_jaxpr/qhk,qhl->kl/dot_general | solution.py:65
  157.0 12.3 %fusion.107 = f32[1024,64]{0,1:T(8,128)} fusion(f32[64,16,1024]{2,1,0:T(8,128)} %fusion.106, f32[1024,64]{0,1:T(8,128)} %get-tuple-element.274, bf16[2,64,16,64]{3,2,1,0:T(8,128)(2,1)} %get-tuple-element.293, s32[]{:T(128)S(6)} %copy.77, pred[]{:T(512)S(6)} %compare.3, f32[64,16,1024]{2,1,0:T(8,128)} %get-tuple-element.258, ...), kind=kOutput, calls=%fused_computation.21.clone.1 | convolution fusion | flops 141690880 | bytes 17629188 | tf_op jit(solution)/shard_map/while/body/eval_jaxpr/qhk,qhr->kr/dot_general | solution.py:71
  169.4 11.3 %fusion.108 = bf16[2,64,16,512]{3,2,1,0:T(8,128)(2,1)} fusion(bf16[2,64,16,512]{3,2,1,0:T(8,128)(2,1)} %get-tuple-element.275, s32[]{:T(128)S(6)} %copy.77, bf16[1024,512]{1,0:T(8,128)(2,1)S(1)} %get-tuple-element.292, f32[64,16,1024]{2,1,0:T(8,128)} %fusion.106, f32[64,16,1024]{2,1,0:T(8,128)} %get-tuple-element.258, f32[64,16]{1,0:T(8,128)} %get-tuple-element.257), kind=kOutput, calls=%fused_computation.18.clone.1 | convolution fusion | flops 1081608192 | bytes 18939908 | tf_op jit(solution)/shard_map/while/body/eval_jaxpr/qhk,kl->qhl/dot_general | solution.py:59
  180.7 11.9 %fusion.109 = bf16[2,64,16,64]{3,2,1,0:T(8,128)(2,1)} fusion(bf16[2,64,16,64]{3,2,1,0:T(8,128)(2,1)} %get-tuple-element.276, s32[]{:T(128)S(6)} %copy.77, f32[64,16,1024]{2,1,0:T(8,128)} %fusion.106, bf16[1024,64]{0,1:T(8,128)(2,1)S(1)} %get-tuple-element.294, f32[64,16,1024]{2,1,0:T(8,128)} %get-tuple-element.258, f32[64,16]{1,0:T(8,128)} %get-tuple-element.257), kind=kOutput, calls=%fused_computation.23.clone.1 | convolution fusion | flops 141625344 | bytes 17235972 | tf_op jit(solution)/shard_map/while/body/eval_jaxpr/qhk,kr->qhr/dot_general | solution.py:62
  195.9 3.8 fusion.104
  199.6 7.3 %fusion.105 = f32[1024,512,1]{1,0,2:T(8,128)} fusion(bf16[2,64,16,512]{3,2,1,0:T(8,128)(2,1)S(1)} %get-tuple-element.295, s32[]{:T(128)S(6)} %copy.77, f32[64,16]{1,0:T(8,128)} %get-tuple-element.257, f32[64,16,1024]{2,1,0:T(8,128)} %copy-done.1), kind=kOutput, calls=%fused_computation.13.clone.1 | convolution fusion | flops 1076889600 | bytes 11567108 | tf_op jit(solution)/shard_map/while/body/eval_jaxpr/qhk,qhl->kl/dot_general | solution.py:68
  206.9 3.3 fusion.106
  210.2 14.8 %bitcast_add_fusion.3 = f32[1024,512]{1,0:T(8,128)} fusion(f32[1024,512,1]{1,0,2:T(8,128)} %fusion.105, f32[1024,512]{1,0:T(8,128)} %get-tuple-element.273, pred[]{:T(512)S(6)} %compare.3, bf16[2,64,16,512]{3,2,1,0:T(8,128)(2,1)} %get-tuple-element.291, s32[]{:T(128)S(6)} %copy.77, f32[64,16,1024]{2,1,0:T(8,128)} %fusion.106, ...), kind=kOutput, calls=%fused_computation.11.clone.1 | convolution fusion | flops 1082656768 | bytes 24182788 | tf_op jit(solution)/shard_map/while/body/eval_jaxpr/qhk,qhl->kl/dot_general | solution.py:65
  225.0 12.3 %fusion.107 = f32[1024,64]{0,1:T(8,128)} fusion(f32[64,16,1024]{2,1,0:T(8,128)} %fusion.106, f32[1024,64]{0,1:T(8,128)} %get-tuple-element.274, bf16[2,64,16,64]{3,2,1,0:T(8,128)(2,1)} %get-tuple-element.293, s32[]{:T(128)S(6)} %copy.77, pred[]{:T(512)S(6)} %compare.3, f32[64,16,1024]{2,1,0:T(8,128)} %get-tuple-element.258, ...), kind=kOutput, calls=%fused_computation.21.clone.1 | convolution fusion | flops 141690880 | bytes 17629188 | tf_op jit(solution)/shard_map/while/body/eval_jaxpr/qhk,qhr->kr/dot_general | solution.py:71
  237.3 11.3 %fusion.108 = bf16[2,64,16,512]{3,2,1,0:T(8,128)(2,1)} fusion(bf16[2,64,16,512]{3,2,1,0:T(8,128)(2,1)} %get-tuple-element.275, s32[]{:T(128)S(6)} %copy.77, bf16[1024,512]{1,0:T(8,128)(2,1)S(1)} %get-tuple-element.292, f32[64,16,1024]{2,1,0:T(8,128)} %fusion.106, f32[64,16,1024]{2,1,0:T(8,128)} %get-tuple-element.258, f32[64,16]{1,0:T(8,128)} %get-tuple-element.257), kind=kOutput, calls=%fused_computation.18.clone.1 | convolution fusion | flops 1081608192 | bytes 18939908 | tf_op jit(solution)/shard_map/while/body/eval_jaxpr/qhk,kl->qhl/dot_general | solution.py:59
  248.6 11.9 %fusion.109 = bf16[2,64,16,64]{3,2,1,0:T(8,128)(2,1)} fusion(bf16[2,64,16,64]{3,2,1,0:T(8,128)(2,1)} %get-tuple-element.276, s32[]{:T(128)S(6)} %copy.77, f32[64,16,1024]{2,1,0:T(8,128)} %fusion.106, bf16[1024,64]{0,1:T(8,128)(2,1)S(1)} %get-tuple-element.294, f32[64,16,1024]{2,1,0:T(8,128)} %get-tuple-element.258, f32[64,16]{1,0:T(8,128)} %get-tuple-element.257), kind=kOutput, calls=%fused_computation.23.clone.1 | convolution fusion | flops 141625344 | bytes 17235972 | tf_op jit(solution)/shard_map/while/body/eval_jaxpr/qhk,kr->qhr/dot_general | solution.py:62
  261.9 12.4 %all_to_all.35 = f32[32,2,1024]{2,1,0:T(2,128)S(1)} all-to-all(f32[32,2,1024]{2,1,0:T(2,128)S(1)} %reshape.172), channel_id=1, replica_groups=mesh['ctx'=32,'head'=8] {'ctx'}, dimensions={0} | all-to-all | bytes 524288 | tf_op jit(solution)/shard_map/all_to_all | solution.py:94
  274.4 3.9 %all-to-all-start.4 = ((f32[32,2,16,512]{3,2,1,0:T(8,128)}), f32[32,2,16,512]{3,2,1,0:T(8,128)S(1)}, u32[]{:S(2)}, u32[]{:S(2)}) async-start(f32[32,2,16,512]{3,2,1,0:T(8,128)} %bitcast.120), calls=%async_computation.4 | async-start | bytes 4194304 | tf_op jit(solution)/shard_map/all_to_all | solution.py:93
  281.8 24.4 %all-to-all-done.4 = f32[32,2,16,512]{3,2,1,0:T(8,128)S(1)} async-done(((f32[32,2,16,512]{3,2,1,0:T(8,128)}), f32[32,2,16,512]{3,2,1,0:T(8,128)S(1)}, u32[]{:S(2)}, u32[]{:S(2)}) %all-to-all-start.4) | async-done | bytes 2097184 | tf_op jit(solution)/shard_map/all_to_all | solution.py:93
  306.2 2.5 broadcast_in_dim.77
  308.7 9.0 %scatter_fusion = f32[128,16,512]{2,1,0:T(8,128)} fusion(f32[128,16,512]{2,1,0:T(8,128)} %broadcast_in_dim.77, s32[64]{0:T(128)S(1)} %fusion.56, f32[64,16,512]{2,1,0:T(8,128)S(1)} %bitcast.117), kind=kCustom, calls=%fused_computation.2 | custom fusion | flops 524288 | bytes 6291712 | tf_op jit(solution)/shard_map/scatter-add | solution.py:100
  317.8 5.8 %copy.67 = f32[128,16,512]{0,1,2:T(8,128)} copy(f32[128,16,512]{2,1,0:T(8,128)} %scatter_fusion) | data formatting | bytes 8388608 | tf_op jit(solution)/shard_map/scatter-add | solution.py:100
  327.1 45.7 %reduce-scatter.3.cloned.1.call-done = f32[128,16,64]{0,1,2:T(8,128)} async-done(((f32[128,16,512]{0,1,2:T(8,128)}), f32[128,16,64]{0,1,2:T(8,128)}) %reduce-scatter.3.cloned.1.call-update) | async-done | bytes 524304 | tf_op jit(solution)/shard_map/reduce_scatter | solution.py:108
  (68 shorter events, 29.6 us)
Async XLA Ops:
  7.2 28.5 %copy-start = (bf16[128,1024]{1,0:T(8,128)(2,1)S(1)}, bf16[128,1024]{1,0:T(8,128)(2,1)}, u32[]{:S(2)}) copy-start(bf16[128,1024]{1,0:T(8,128)(2,1)} %param.13) | copy-start | bytes 786436
  24.4 11.3 %copy-start.6 = (s32[32,1,2]{2,1,0:T(1,128)}, s32[32,1,2]{2,1,0:T(1,128)S(1)}, u32[]{:S(2)}) copy-start(s32[32,1,2]{2,1,0:T(1,128)S(1)} %all_to_all.34) | copy-start | bytes 772
  27.2 56.6 %all-to-all-start = ((bf16[8,128,16,64]{1,3,2,0:T(8,128)(2,1)}), bf16[8,128,16,64]{1,3,2,0:T(8,128)(2,1)S(1)}, u32[]{:S(2)}, u32[]{:S(2)}) async-start(bf16[8,128,16,64]{1,3,2,0:T(8,128)(2,1)} %stack.2), calls=%async_computation | async-start | bytes 4194304 | tf_op jit(solution)/shard_map/all_to_all | solution.py:27
  83.8 16.8 %all-to-all-start.3 = ((bf16[32,2,1024]{2,1,0:T(2,128)(2,1)}), bf16[32,2,1024]{2,1,0:T(2,128)(2,1)S(1)}, u32[]{:S(2)}, u32[]{:S(2)}) async-start(bf16[32,2,1024]{2,1,0:T(2,128)(2,1)} %reshape.183), calls=%async_computation.3 | async-start | bytes 262144 | tf_op jit(solution)/shard_map/all_to_all | solution.py:31
  97.2 28.0 %copy-start.2 = (bf16[128,16,512]{2,1,0:T(8,128)(2,1)S(1)}, bf16[128,16,512]{2,1,0:T(8,128)(2,1)}, u32[]{:S(2)}) copy-start(bf16[128,16,512]{2,1,0:T(8,128)(2,1)} %param.14) | copy-start | bytes 6291460
  100.6 24.7 %all-to-all-start.2 = ((bf16[32,2,16,512]{3,2,1,0:T(8,128)(2,1)}), bf16[32,2,16,512]{3,2,1,0:T(8,128)(2,1)S(1)}, u32[]{:S(2)}, u32[]{:S(2)}) async-start(bf16[32,2,16,512]{3,2,1,0:T(8,128)(2,1)} %bitcast.119), calls=%async_computation.2 | async-start | bytes 2097152 | tf_op jit(solution)/shard_map/all_to_all | solution.py:30
  125.2 1.8 copy-start.4
  125.2 1.8 copy-start.3
  128.5 3.8 copy-start.1
  192.6 1.8 copy-start.4
  192.6 1.8 copy-start.3
  195.9 3.8 copy-start.1
  260.5 18.3 %copy-start.7 = (s32[32,1,2]{2,1,0:T(1,128)S(1)}, s32[32,1,2]{2,1,0:T(1,128)}, u32[]{:S(2)}) copy-start(s32[32,1,2]{2,1,0:T(1,128)} %copy-done.6) | copy-start | bytes 772
  274.4 31.9 %all-to-all-start.4 = ((f32[32,2,16,512]{3,2,1,0:T(8,128)}), f32[32,2,16,512]{3,2,1,0:T(8,128)S(1)}, u32[]{:S(2)}, u32[]{:S(2)}) async-start(f32[32,2,16,512]{3,2,1,0:T(8,128)} %bitcast.120), calls=%async_computation.4 | async-start | bytes 4194304 | tf_op jit(solution)/shard_map/all_to_all | solution.py:93
  278.3 47.4 %reduce-scatter.5.cloned.1.call-start = ((), (), s32[]{:S(2)}) async-start(), calls=%async_computation.9 | async-start | bytes 589824 | tf_op jit(solution)/shard_map/reduce_scatter | solution.py:109
  281.8 91.1 %reduce-scatter.3.cloned.1.call-start = ((), (), s32[]{:S(2)}) async-start(), calls=%async_computation.8 | async-start | bytes 4718592 | tf_op jit(solution)/shard_map/reduce_scatter | solution.py:108
  323.6 1.0 copy-start.5
Sparse Core Ops, SparseCore 0:
  281.9 29.2 reduce-scatter.4
  323.7 49.0 reduce-scatter.2
